TPU v7x, 512 devices: a whole 4x8x8 slice. The times are simulated.
512 devices in a mesh: dp: 16 (over y, core), tensor: 32 (over z, x).
Axes of the slice: x: 4, y: 8, z: 8, core: 2. Of those that a mesh axis runs over, the one named last changes fastest.
Arguments:
- tokens: bfloat16 [2048, 4096], P('dp', 'tensor'), may hold values from -6 to 6
- gate_pre: bfloat16 [2048, 16384], P('dp', 'tensor'), may hold values from -6 to 6
- up_blocks: bfloat16 [32, 64, 128, 128], P('tensor'), may hold values from -0.125 to 0.125
- up_mask: int32 [32, 128], P(None, 'tensor'), may hold values from 0 to 1, as said below
- down_blocks: bfloat16 [32, 64, 128, 128], P('tensor'), may hold values from -0.0625 to 0.0625
- down_mask: int32 [128, 32], replicated, may hold values from 0 to 1, as said below
- down_owner: int32 [128], replicated, may hold values from 0 to 31, as said below
- cotangent: bfloat16 [2048, 4096], P('dp', 'tensor'), may hold values from -6 to 6
Outputs:
- mixed: bfloat16 [2048, 4096], P('dp', 'tensor')
- input_grad: bfloat16 [2048, 4096], P('dp', 'tensor')
- gate_grad: bfloat16 [2048, 16384], P('dp', 'tensor')
- up_grad: bfloat16 [32, 64, 128, 128], P('tensor', 'dp')
- down_grad: bfloat16 [32, 64, 128, 128], P('tensor', 'dp')
Inputs may be any that keep to these rules, and one draw needn't show every extreme that they name: `up_mask`: each column strip of 4 block columns holds exactly 64 ones. `down_mask`: the rows owned by one device hold exactly 64 ones together. `down_owner`: every device owns exactly 4 block rows.
All inputs are finite; a program needn't handle non-finite values.
Results may differ from a plain program's by a relative error of at most 0.022.
Values may be sent and summed in bfloat16 or wider, within the bound.
No kernel may reach another device: no remote copies, remote signals or barrier semaphores. Data moves between devices by JAX's collectives and lax.ppermute only.
A program may use at most 128 MiB of HBM per device.

v0:
```python
import jax
import jax.numpy as jnp
from jax import lax
from jax.sharding import PartitionSpec as P


def kept_positions(marked, total):
    marked = marked.reshape(-1).astype(jnp.int32)
    running = jnp.cumsum(marked) - 1
    target = jnp.where(marked > 0, running, total)
    indices = jnp.arange(marked.shape[0], dtype=jnp.int32)
    return jnp.zeros((total,), jnp.int32).at[target].set(indices, mode="drop")


def one_hot(indices, total):
    return (indices[:, None] == jnp.arange(total, dtype=jnp.int32)[None, :]).astype(jnp.float32)


def row_slots(down_owner, devices):
    marks = (down_owner[:, None] == jnp.arange(devices, dtype=jnp.int32)[None, :]).astype(jnp.int32)
    earlier = jnp.cumsum(marks, axis=0) - marks
    return jnp.sum(earlier * marks, axis=1)


def picker(wanted, block, current, segment):
    block_count = segment.shape[1] // block
    inside = (wanted >= 0) & (wanted < block_count)
    shaped = segment.reshape(segment.shape[0], block_count, block)
    chosen = jnp.take(shaped, jnp.clip(wanted, 0, block_count - 1), axis=1)
    return jnp.where(inside[None, :, None], chosen, current)


def shards(tokens, gate_pre, up_blocks, up_mask, down_blocks, down_mask, down_owner, cotangent):
    devices = lax.axis_size("tensor")
    position = lax.axis_index("tensor")
    token_count = tokens.shape[0]
    blocks_wide = up_mask.shape[0]
    strip_size = up_mask.shape[1]
    block = up_blocks.shape[2]
    kept_up = up_blocks.shape[1]
    kept_down = down_blocks.shape[1]
    model_width = blocks_wide * block
    highest = lax.Precision.HIGHEST
    x_full, dy_full = (
        lax.all_gather(tokens, "tensor", axis=1, tiled=True),
        lax.all_gather(cotangent, "tensor", axis=1, tiled=True),
    )
    token_blocks = x_full.reshape(token_count, blocks_wide, block)
    cot_blocks = dy_full.reshape(token_count, blocks_wide, block)
    w_up = up_blocks[0]
    w_down = down_blocks[0]
    up_pos = kept_positions(up_mask, kept_up)
    up_rows = up_pos // strip_size
    up_cols = up_pos % strip_size
    token_chosen = jnp.take(token_blocks, up_rows, axis=1)
    product = jnp.einsum("nkb,kbc->nkc", token_chosen, w_up, preferred_element_type=jnp.float32)
    up_val = jnp.einsum("nkc,ks->nsc", product, one_hot(up_cols, strip_size), precision=highest)
    gate_val = gate_pre.reshape(token_count, strip_size, block).astype(jnp.float32)
    sigmoid_gate = jax.nn.sigmoid(gate_val)
    activated = gate_val * sigmoid_gate
    hidden = (activated * up_val).astype(jnp.bfloat16).reshape(token_count, strip_size * block)
    my_rows = kept_positions(down_owner == position, strip_size)
    owned_mask = jnp.take(down_mask, my_rows, axis=0)
    down_pos = kept_positions(owned_mask, kept_down)
    slots = down_pos // blocks_wide
    down_cols = down_pos % blocks_wide
    empty = jnp.zeros((token_count, strip_size, block), jnp.bfloat16)
    hidden_owned = picker(
        my_rows, block, empty, lax.all_gather(hidden, "tensor", axis=1, tiled=True)
    )
    h_chosen = jnp.take(hidden_owned, slots, axis=1)
    product = jnp.einsum("nkb,kbc->nkc", h_chosen, w_down, preferred_element_type=jnp.float32)
    out_part = jnp.einsum(
        "nkc,kj->njc", product, one_hot(down_cols, blocks_wide), precision=highest
    )
    out_part = out_part.astype(jnp.bfloat16).reshape(1, token_count, model_width)
    dy_chosen = jnp.take(cot_blocks, down_cols, axis=1)
    down_term = jnp.einsum("nkb,nkc->kbc", h_chosen, dy_chosen, preferred_element_type=jnp.float32)[
        None
    ]
    backward = jnp.einsum("nkc,kbc->nkb", dy_chosen, w_down, preferred_element_type=jnp.float32)
    dh_owned = jnp.einsum("nkb,ka->nab", backward, one_hot(slots, strip_size), precision=highest)
    dh_owned = dh_owned.astype(jnp.bfloat16).reshape(token_count, strip_size * block)
    home_index = down_owner * strip_size + row_slots(down_owner, devices)
    targets = position * strip_size + jnp.arange(strip_size, dtype=jnp.int32)
    wanted = jnp.take(home_index, targets)
    hidden_grad = picker(
        wanted, block, empty, lax.all_gather(dh_owned, "tensor", axis=1, tiled=True)
    )
    dh_float = hidden_grad.astype(jnp.float32)
    gate_grad = (dh_float * up_val * sigmoid_gate * (1.0 + gate_val * (1.0 - sigmoid_gate))).astype(
        jnp.bfloat16
    )
    gate_grad = gate_grad.reshape(token_count, strip_size * block)
    up_act_grad = (dh_float * activated).astype(jnp.bfloat16)
    du_chosen = jnp.take(up_act_grad, up_cols, axis=1)
    product = jnp.einsum("nkc,kbc->nkb", du_chosen, w_up, preferred_element_type=jnp.float32)
    in_part = jnp.einsum("nkb,kr->nrb", product, one_hot(up_rows, blocks_wide), precision=highest)
    in_part = in_part.astype(jnp.bfloat16).reshape(1, token_count, model_width)
    up_term = jnp.einsum(
        "nkb,nkc->kbc", token_chosen, du_chosen, preferred_element_type=jnp.float32
    )[None]
    out_pieces, in_pieces = (
        lax.all_to_all(out_part, "tensor", split_axis=2, concat_axis=0, tiled=True),
        lax.all_to_all(in_part, "tensor", split_axis=2, concat_axis=0, tiled=True),
    )
    mixed = jnp.sum(out_pieces.astype(jnp.float32), axis=0).astype(jnp.bfloat16)
    input_grad = jnp.sum(in_pieces.astype(jnp.float32), axis=0).astype(jnp.bfloat16)
    up_sum, down_sum = (
        lax.psum_scatter(
            up_term.astype(jnp.bfloat16), "dp", scatter_dimension=1, tiled=True
        ).astype(jnp.float32),
        lax.psum_scatter(
            down_term.astype(jnp.bfloat16), "dp", scatter_dimension=1, tiled=True
        ).astype(jnp.float32),
    )
    up_grad = up_sum.astype(jnp.bfloat16)
    down_grad = down_sum.astype(jnp.bfloat16)
    return (mixed, input_grad, gate_grad, up_grad, down_grad)


def solution(mesh):
    placed = (
        P("dp", "tensor"),
        P("dp", "tensor"),
        P("tensor", None, None, None),
        P(None, "tensor"),
        P("tensor", None, None, None),
        P(),
        P(),
        P("dp", "tensor"),
    )
    return jax.shard_map(
        shards,
        mesh=mesh,
        in_specs=placed,
        out_specs=(
            P("dp", "tensor"),
            P("dp", "tensor"),
            P("dp", "tensor"),
            P("tensor", "dp", None, None),
            P("tensor", "dp", None, None),
        ),
        check_vma=False,
    )
```

profile of v0, /device:TPU:2, one launch (start us, length us, event | category | flops | bytes accessed | tf_op | source)
XLA Modules:
  0.0 517.0 jit_solution(11576796951660111175)
XLA Ops:
  18.4 79.6 %all-gather.9.cloned.1.call-done = bf16[128,4096]{0,1:T(8,128)(2,1)} async-done(((bf16[128,128]{0,1:T(8,128)(2,1)}), bf16[128,4096]{0,1:T(8,128)(2,1)}) %all-gather.9.cloned.1.call-update) | async-done | bytes 1048592 | tf_op jit(solution)/shard_map/all_gather | solution.py:46
  99.6 2.2 gather_fusion.5
  101.8 3.8 convolution_bitcast_fusion.1
  105.7 3.8 fusion.48
  115.2 66.1 %all-gather.5.cloned.1.call-done = bf16[128,4096]{0,1:T(8,128)(2,1)} async-done(((bf16[128,128]{0,1:T(8,128)(2,1)}), bf16[128,4096]{0,1:T(8,128)(2,1)}) %all-gather.5.cloned.1.call-update) | async-done | bytes 1048592 | tf_op jit(solution)/shard_map/all_gather | solution.py:45
  182.9 2.2 gather_fusion.2
  185.0 4.3 convolution_bitcast_fusion.3
  189.4 80.9 %all-gather.11.cloned.1.call-done = bf16[128,16384]{0,1:T(8,128)(2,1)} async-done(((bf16[128,512]{0,1:T(8,128)(2,1)}), bf16[128,16384]{0,1:T(8,128)(2,1)}) %all-gather.11.cloned.1.call-update) | async-done | bytes 4194320 | tf_op jit(solution)/shard_map/all_gather | solution.py:88
  270.3 6.4 %copy.134 = bf16[128,128,128]{2,0,1:T(8,128)(2,1)} copy(bf16[128,128,128]{0,2,1:T(8,128)(2,1)} %bitcast.106) | data formatting | bytes 8388608 | tf_op jit(solution)/shard_map/reshape | solution.py:28
  276.7 2.8 gather_fusion.6
  279.4 6.0 %fusion.54 = (bf16[128,4,128]{2,1,0:T(4,128)(2,1)S(1)}, bf16[128,4,128]{2,1,0:T(4,128)(2,1)S(1)}, bf16[128,4,128]{2,1,0:T(4,128)(2,1)S(1)}) fusion(f32[128,4,128]{2,1,0:T(4,128)S(1)} %reshape.234, bf16[4,128,128]{2,1,0:T(8,128)(2,1)S(1)} %gather_fusion.6, pred[4]{0:T(512)(128)(4,1)S(1)} %copy-done.17, pred[4]{0:T(512)(128)(4,1)S(1)} %copy-done.16, ...), kind=kOutput, calls=%fused_computation.55 | convolution fusion | flops 51511552 | bytes 4981000 | tf_op jit(solution)/shard_map/nkc,ks->nsc/dot_general | solution.py:57
  286.4 2.2 gather_fusion.7
  288.6 4.6 convert_bitcast_fusion.1
  293.9 5.2 %convolution_bitcast_fusion = f32[128,64,128]{2,0,1:T(8,128)} fusion(bf16[1,64,128,128]{3,2,1,0:T(8,128)(2,1)S(1)} %copy-done, bf16[64,128,128]{2,1,0:T(8,128)(2,1)} %gather_fusion.7, pred[64]{0:T(512)(128)(4,1)S(1)} %copy-done.6), kind=kOutput, calls=%fused_computation.19 | convolution fusion | flops 269484032 | bytes 8388672 | tf_op jit(solution)/shard_map/nkc,kbc->nkb/dot_general | solution.py:97
  299.1 72.1 %all-gather.7.cloned.1.call-done = bf16[128,16384]{0,1:T(8,128)(2,1)} async-done(((bf16[128,512]{0,1:T(8,128)(2,1)}), bf16[128,16384]{0,1:T(8,128)(2,1)}) %all-gather.7.cloned.1.call-update) | async-done | bytes 4194320 | tf_op jit(solution)/shard_map/all_gather | solution.py:69
  371.2 6.5 %copy.125 = bf16[128,128,128]{2,0,1:T(8,128)(2,1)} copy(bf16[128,128,128]{0,2,1:T(8,128)(2,1)} %bitcast.107) | data formatting | bytes 8388608 | tf_op jit(solution)/shard_map/reshape | solution.py:28
  377.7 2.8 gather_fusion.3
  380.6 2.1 gather_fusion.4
  382.8 4.6 convert_bitcast_fusion
  387.9 6.1 %fusion.36 = bf16[128,32,128]{2,1,0:T(8,128)(2,1)S(1)} fusion(f32[128,64,128]{2,0,1:T(8,128)} %convolution_bitcast_fusion, s32[64]{0:T(128)S(1)} %copy-done.14), kind=kOutput, calls=%fused_computation.45 | convolution fusion | flops 403179520 | bytes 5243136 | tf_op jit(solution)/shard_map/nkb,kr->nrb/dot_general | solution.py:98
  394.5 2.8 copy.138
  397.9 22.4 %reduce.15 = bf16[4096,128]{1,0:T(8,128)(2,1)S(1)} reduce(bf16[4096,1,128]{2,1,0:T(2,128)(2,1)S(1)} %bitcast.102, bf16[]{:T(256)} %broadcast.484), dimensions={1}, to_apply=%bitcast.95.reduce_sub_computation | reduce | bytes 2097154
  421.4 7.0 %all-to-all-start.1 = ((bf16[32,2,8192]{2,1,0:T(2,128)(2,1)}), bf16[32,2,8192]{2,1,0:T(2,128)(2,1)S(1)}, u32[]{:S(2)}, u32[]{:S(2)}) async-start(bf16[32,2,8192]{2,1,0:T(2,128)(2,1)} %reshape.359), calls=%async_computation.1 | async-start | bytes 2097152 | tf_op jit(solution)/shard_map/all_to_all | solution.py:105
  428.4 2.4 convolution_bitcast_fusion.2
  430.8 4.1 fusion.39
  436.2 5.0 copy.129
  441.2 23.4 %reduce.14 = bf16[4096,128]{1,0:T(8,128)(2,1)} reduce(bf16[4096,1,128]{2,1,0:T(2,128)(2,1)S(1)} %bitcast.103, bf16[]{:T(256)} %broadcast.484), dimensions={1}, to_apply=%bitcast.93.reduce_sub_computation | reduce | bytes 2097154
  464.6 2.1 reshape.357
  466.7 9.8 %all-to-all-start = ((bf16[32,2,8192]{2,1,0:T(2,128)(2,1)}), bf16[32,2,8192]{2,1,0:T(2,128)(2,1)}, u32[]{:S(2)}, u32[]{:S(2)}) async-start(bf16[32,2,8192]{2,1,0:T(2,128)(2,1)} %reshape.357), calls=%async_computation | async-start | bytes 2097152 | tf_op jit(solution)/shard_map/all_to_all | solution.py:104
  479.3 22.0 %all-to-all-done = bf16[32,2,8192]{2,1,0:T(2,128)(2,1)} async-done(((bf16[32,2,8192]{2,1,0:T(2,128)(2,1)}), bf16[32,2,8192]{2,1,0:T(2,128)(2,1)}, u32[]{:S(2)}, u32[]{:S(2)}) %all-to-all-start) | async-done | bytes 1048608 | tf_op jit(solution)/shard_map/all_to_all | solution.py:104
  501.3 5.8 %reshape.358 = bf16[4096,1,128]{2,1,0:T(2,128)(2,1)} reshape(bf16[32,2,8192]{2,1,0:T(2,128)(2,1)} %all-to-all-done) | data formatting | bytes 2097152
  507.1 1.9 copy.147
  (116 shorter events, 29.3 us)
Async XLA Ops:
  7.2 177.9 %copy-start = (bf16[1,64,128,128]{3,2,1,0:T(8,128)(2,1)S(1)}, bf16[1,64,128,128]{3,2,1,0:T(8,128)(2,1)}, u32[]{:S(2)}) copy-start(bf16[1,64,128,128]{3,2,1,0:T(8,128)(2,1)} %param.16) | copy-start | bytes 6291460
  7.2 90.8 %all-gather.9.cloned.1.call-start = ((), (), s32[]{:S(2)}) async-start(), calls=%async_computation.6 | async-start | bytes 1081344 | tf_op jit(solution)/shard_map/all_gather | solution.py:46
  8.9 172.4 %all-gather.5.cloned.1.call-start = ((), (), s32[]{:S(2)}) async-start(), calls=%async_computation.4 | async-start | bytes 1081344 | tf_op jit(solution)/shard_map/all_gather | solution.py:45
  10.4 259.9 %all-gather.11.cloned.1.call-start = ((), (), s32[]{:S(2)}) async-start(), calls=%async_computation.7 | async-start | bytes 4325376 | tf_op jit(solution)/shard_map/all_gather | solution.py:88
  18.3 83.5 %copy-start.11 = (s32[64]{0:T(128)}, s32[64]{0:T(128)S(1)}, u32[]{:S(2)}) copy-start(s32[64]{0:T(128)S(1)} %get-tuple-element.20) | copy-start | bytes 772
  18.3 87.3 %copy-start.4 = (s32[64]{0:T(128)}, s32[64]{0:T(128)S(1)}, u32[]{:S(2)}) copy-start(s32[64]{0:T(128)S(1)} %get-tuple-element.33) | copy-start | bytes 772
  105.6 4.7 copy-start.9
  105.7 5.0 copy-start.3
  110.3 260.9 %all-gather.7.cloned.1.call-start = ((), (), s32[]{:S(2)}) async-start(), calls=%async_computation.5 | async-start | bytes 4325376 | tf_op jit(solution)/shard_map/all_gather | solution.py:69
  114.6 0.5 copy-start.13
  114.6 70.4 %copy-start.7 = (pred[64]{0:T(512)(128)(4,1)}, pred[64]{0:T(512)(128)(4,1)S(1)}, u32[]{:S(2)}) copy-start(pred[64]{0:T(512)(128)(4,1)S(1)} %get-tuple-element.38) | copy-start | bytes 196
  270.3 9.2 %copy-start.15 = (s32[64]{0:T(128)S(1)}, s32[64]{0:T(128)}, u32[]{:S(2)}) copy-start(s32[64]{0:T(128)} %get-tuple-element.14) | copy-start | bytes 772
  270.3 9.2 %copy-start.16 = (pred[4]{0:T(512)(128)(4,1)S(1)}, pred[4]{0:T(512)(128)(4,1)}, u32[]{:S(2)}) copy-start(pred[4]{0:T(512)(128)(4,1)} %get-tuple-element.15) | copy-start | bytes 16
  270.3 9.2 %copy-start.17 = (pred[4]{0:T(512)(128)(4,1)S(1)}, pred[4]{0:T(512)(128)(4,1)}, u32[]{:S(2)}) copy-start(pred[4]{0:T(512)(128)(4,1)} %get-tuple-element.17) | copy-start | bytes 16
  286.3 223.6 %reduce-scatter.3.cloned.1.call-start = ((), (), s32[]{:S(2)}) async-start(), calls=%async_computation.8 | async-start | bytes 2228224 | tf_op jit(solution)/shard_map/reduce_scatter | solution.py:110
  286.4 2.2 copy-start.6
  286.4 2.2 copy-start.8
  293.2 0.7 copy-start.10
  293.2 0.7 copy-start.5
  293.2 216.7 %reduce-scatter.5.cloned.1.call-start = ((), (), s32[]{:S(2)}) async-start(), calls=%async_computation.9 | async-start | bytes 2228224 | tf_op jit(solution)/shard_map/reduce_scatter | solution.py:113
  387.3 0.6 copy-start.14
  420.2 8.2 %copy-start.2 = (bf16[64,128,128]{2,1,0:T(8,128)(2,1)S(1)}, bf16[64,128,128]{2,1,0:T(8,128)(2,1)}, u32[]{:S(2)}) copy-start(bf16[64,128,128]{2,1,0:T(8,128)(2,1)} %gather_fusion.4) | copy-start | bytes 6291460
  421.4 45.4 %all-to-all-start.1 = ((bf16[32,2,8192]{2,1,0:T(2,128)(2,1)}), bf16[32,2,8192]{2,1,0:T(2,128)(2,1)S(1)}, u32[]{:S(2)}, u32[]{:S(2)}) async-start(bf16[32,2,8192]{2,1,0:T(2,128)(2,1)} %reshape.359), calls=%async_computation.1 | async-start | bytes 2097152 | tf_op jit(solution)/shard_map/all_to_all | solution.py:105
  428.4 2.4 copy-start.12
  466.7 34.6 %all-to-all-start = ((bf16[32,2,8192]{2,1,0:T(2,128)(2,1)}), bf16[32,2,8192]{2,1,0:T(2,128)(2,1)}, u32[]{:S(2)}, u32[]{:S(2)}) async-start(bf16[32,2,8192]{2,1,0:T(2,128)(2,1)} %reshape.357), calls=%async_computation | async-start | bytes 2097152 | tf_op jit(solution)/shard_map/all_to_all | solution.py:104
  507.1 2.8 copy-start.1
Sparse Core Ops, SparseCore 0:
  11.8 86.1 all-gather.8
  101.7 79.5 all-gather.4
  185.0 85.2 all-gather.10
  286.4 84.7 all-gather.6
  374.4 59.0 reduce-scatter.2
  436.8 61.4 reduce-scatter.4
where the time goes:
time: 525 us; the launch traced here: 517 us
  waiting for transfers between devices  321 us (61%)
  local copies, waits for them, and re-layouts  67 us (13%)
  other arithmetic  52.4 us (10%)
  matrix products  44.8 us (9%)
  starting transfers between devices  17.1 us (3%)
  between operations  14.8 us (3%)
    all_gather x1, waiting for transfers between devices, shards(): lax.all_gather(dh_owned, 'tensor', axis=1, tiled=True)  80.9 us
    all_gather x1, waiting for transfers between devices, shards(): lax.all_gather(cotangent, 'tensor', axis=1, tiled=True)  79.6 us
    all_gather x1, waiting for transfers between devices, shards(): lax.all_gather(hidden, 'tensor', axis=1, tiled=True)  72.1 us
    all_gather x1, waiting for transfers between devices, shards(): lax.all_gather(tokens, 'tensor', axis=1, tiled=True)  66.1 us
    unnamed x2, other arithmetic  45.8 us
    all_to_all x1, waiting for transfers between devices, shards(): lax.all_to_all(out_part, 'tensor', split_axis=2, concat_axis=0, tiled=True)  22 us
    unnamed x50, local copies, waits for them, and re-layouts  20.5 us
    reshape x2, local copies, waits for them, and re-layouts, picker(): shaped = segment.reshape(segment.shape[0], block_count, block)  12.9 us
  transfers between devices with their start and end apart: 8, of which 5 were waited for; matrix products, arithmetic and copies ran while one was open for 28% of the time, Pallas kernels for 0%

commit v1 on v0

--- a/solution.py
+++ b/solution.py
@@ -2,6 +2,11 @@
 import jax.numpy as jnp
 from jax import lax
 from jax.sharding import PartitionSpec as P
+
+
+def gather_from_all(shard, axis, dim):
+    copies = jnp.concatenate([shard] * lax.axis_size(axis), axis=dim)
+    return lax.all_to_all(copies, axis, dim, dim, tiled=True)
 
 
 def kept_positions(marked, total):
@@ -65,9 +70,7 @@
     slots = down_pos // blocks_wide
     down_cols = down_pos % blocks_wide
     empty = jnp.zeros((token_count, strip_size, block), jnp.bfloat16)
-    hidden_owned = picker(
-        my_rows, block, empty, lax.all_gather(hidden, "tensor", axis=1, tiled=True)
-    )
+    hidden_owned = picker(my_rows, block, empty, gather_from_all(hidden, "tensor", 1))
     h_chosen = jnp.take(hidden_owned, slots, axis=1)
     product = jnp.einsum("nkb,kbc->nkc", h_chosen, w_down, preferred_element_type=jnp.float32)
     out_part = jnp.einsum(

time: 525 us -> 540 us (1.029)
  waiting for transfers between devices: 321 us -> 329 us
  starting transfers between devices: 17.1 us -> 22.6 us
    all_to_all x0 -> x1, waiting for transfers between devices: none -> 80.1 us  [gather_from_all(): return lax.all_to_all(copies, axis, dim, dim, tiled=True)]
    all_gather x1 -> x0, waiting for transfers between devices: 72.1 us -> none  [shards(): lax.all_gather(hidden, 'tensor', axis=1, tiled=True)]
    all_to_all x0 -> x1, starting transfers between devices: none -> 6.71 us  [gather_from_all(): return lax.all_to_all(copies, axis, dim, dim, tiled=True)]
  transfers between devices with their start and end apart: 8 -> 8, of which waited for: 5 -> 5; matrix products, arithmetic and copies ran while one was open for 28% -> 27% of each run, Pallas kernels for 0% -> 0%
where the time goes in v1:
time: 540 us; the launch traced here: 532 us
  waiting for transfers between devices  329 us (61%)
  local copies, waits for them, and re-layouts  69.2 us (13%)
  other arithmetic  52.4 us (10%)
  matrix products  44.8 us (8%)
  starting transfers between devices  22.6 us (4%)
  between operations  14.5 us (3%)
    all_gather x1, waiting for transfers between devices, shards(): lax.all_gather(dh_owned, 'tensor', axis=1, tiled=True)  80.9 us
    all_to_all x1, waiting for transfers between devices, gather_from_all(): return lax.all_to_all(copies, axis, dim, dim, tiled=True)  80.1 us
    all_gather x1, waiting for transfers between devices, shards(): lax.all_gather(cotangent, 'tensor', axis=1, tiled=True)  79.6 us
    all_gather x1, waiting for transfers between devices, shards(): lax.all_gather(tokens, 'tensor', axis=1, tiled=True)  66.1 us
    unnamed x2, other arithmetic  45.8 us
    all_to_all x1, waiting for transfers between devices, shards(): lax.all_to_all(out_part, 'tensor', split_axis=2, concat_axis=0, tiled=True)  21.8 us
    unnamed x50, local copies, waits for them, and re-layouts  20.5 us
    reshape x2, local copies, waits for them, and re-layouts, picker(): shaped = segment.reshape(segment.shape[0], block_count, block)  12.9 us
  transfers between devices with their start and end apart: 8, of which 5 were waited for; matrix products, arithmetic and copies ran while one was open for 27% of the time, Pallas kernels for 0%

profile of v1, /device:TPU:2, one launch (start us, length us, event | category | flops | bytes accessed | tf_op | source)
XLA Modules:
  0.0 532.2 jit_solution(13104569155045284431)
XLA Ops:
  18.4 79.6 %all-gather.6.cloned.1.call-done = bf16[128,4096]{0,1:T(8,128)(2,1)} async-done(((bf16[128,128]{0,1:T(8,128)(2,1)}), bf16[128,4096]{0,1:T(8,128)(2,1)}) %all-gather.6.cloned.1.call-update) | async-done | bytes 1048592 | tf_op jit(solution)/shard_map/all_gather | solution.py:51
  99.6 2.2 gather_fusion.5
  101.8 3.8 convolution_bitcast_fusion.1
  105.7 3.8 fusion.48
  115.1 66.1 %all-gather.4.cloned.1.call-done = bf16[128,4096]{0,1:T(8,128)(2,1)} async-done(((bf16[128,128]{0,1:T(8,128)(2,1)}), bf16[128,4096]{0,1:T(8,128)(2,1)}) %all-gather.4.cloned.1.call-update) | async-done | bytes 1048592 | tf_op jit(solution)/shard_map/all_gather | solution.py:50
  182.9 2.2 gather_fusion.2
  185.0 4.3 convolution_bitcast_fusion.3
  189.4 80.9 %all-gather.8.cloned.1.call-done = bf16[128,16384]{0,1:T(8,128)(2,1)} async-done(((bf16[128,512]{0,1:T(8,128)(2,1)}), bf16[128,16384]{0,1:T(8,128)(2,1)}) %all-gather.8.cloned.1.call-update) | async-done | bytes 4194320 | tf_op jit(solution)/shard_map/all_gather | solution.py:91
  270.3 6.4 %copy.134 = bf16[128,128,128]{2,0,1:T(8,128)(2,1)} copy(bf16[128,128,128]{0,2,1:T(8,128)(2,1)} %bitcast.106) | data formatting | bytes 8388608 | tf_op jit(solution)/shard_map/reshape | solution.py:33
  276.7 2.8 gather_fusion.6
  279.4 6.0 %fusion.54 = (bf16[128,4,128]{2,1,0:T(4,128)(2,1)S(1)}, bf16[128,4,128]{2,1,0:T(4,128)(2,1)S(1)}, bf16[128,4,128]{2,1,0:T(4,128)(2,1)S(1)}) fusion(f32[128,4,128]{2,1,0:T(4,128)S(1)} %reshape.300, bf16[4,128,128]{2,1,0:T(8,128)(2,1)S(1)} %gather_fusion.6, pred[4]{0:T(512)(128)(4,1)S(1)} %copy-done.17, pred[4]{0:T(512)(128)(4,1)S(1)} %copy-done.16, ...), kind=kOutput, calls=%fused_computation.55 | convolution fusion | flops 51511552 | bytes 4981000 | tf_op jit(solution)/shard_map/nkc,ks->nsc/dot_general | solution.py:62
  285.6 2.9 concatenate.7
  288.6 6.7 %all-to-all-start = ((bf16[128,32,512]{0,2,1:T(8,128)(2,1)}), bf16[128,32,512]{0,2,1:T(8,128)(2,1)}, u32[]{:S(2)}, u32[]{:S(2)}) async-start(bf16[128,32,512]{0,2,1:T(8,128)(2,1)} %concatenate.7), calls=%async_computation | async-start | bytes 8388608 | tf_op jit(solution)/shard_map/all_to_all | solution.py:9
  295.4 2.1 gather_fusion.7
  297.5 4.6 convert_bitcast_fusion.1
  302.8 5.2 convolution_bitcast_fusion
  308.0 80.1 %all-to-all-done = bf16[128,32,512]{0,2,1:T(8,128)(2,1)} async-done(((bf16[128,32,512]{0,2,1:T(8,128)(2,1)}), bf16[128,32,512]{0,2,1:T(8,128)(2,1)}, u32[]{:S(2)}, u32[]{:S(2)}) %all-to-all-start) | async-done | bytes 4194336 | tf_op jit(solution)/shard_map/all_to_all | solution.py:9
  388.1 6.5 %copy.125 = bf16[128,128,128]{2,0,1:T(8,128)(2,1)} copy(bf16[128,128,128]{0,2,1:T(8,128)(2,1)} %bitcast.9) | data formatting | bytes 8388608 | tf_op jit(solution)/shard_map/reshape | solution.py:33
  394.6 2.8 gather_fusion.3
  399.6 4.6 convert_bitcast_fusion
  404.8 6.1 %fusion.36 = bf16[128,32,128]{2,1,0:T(8,128)(2,1)S(1)} fusion(f32[128,64,128]{2,0,1:T(8,128)} %convolution_bitcast_fusion, s32[64]{0:T(128)S(1)} %copy-done.14), kind=kOutput, calls=%fused_computation.45 | convolution fusion | flops 403179520 | bytes 5243136 | tf_op jit(solution)/shard_map/nkb,kr->nrb/dot_general | solution.py:101
  411.4 2.8 copy.138
  414.7 22.4 %reduce.15 = bf16[4096,128]{1,0:T(8,128)(2,1)S(1)} reduce(bf16[4096,1,128]{2,1,0:T(2,128)(2,1)S(1)} %bitcast.102, bf16[]{:T(256)} %broadcast.485), dimensions={1}, to_apply=%bitcast.95.reduce_sub_computation | reduce | bytes 2097154
  438.3 5.9 %all-to-all-start.2 = ((bf16[32,2,8192]{2,1,0:T(2,128)(2,1)}), bf16[32,2,8192]{2,1,0:T(2,128)(2,1)S(1)}, u32[]{:S(2)}, u32[]{:S(2)}) async-start(bf16[32,2,8192]{2,1,0:T(2,128)(2,1)} %reshape.425), calls=%async_computation.2 | async-start | bytes 2097152 | tf_op jit(solution)/shard_map/all_to_all | solution.py:108
  444.2 2.4 convolution_bitcast_fusion.2
  446.6 4.1 fusion.39
  451.9 5.0 copy.129
  457.0 23.4 %reduce.14 = bf16[4096,128]{1,0:T(8,128)(2,1)} reduce(bf16[4096,1,128]{2,1,0:T(2,128)(2,1)S(1)} %bitcast.103, bf16[]{:T(256)} %broadcast.485), dimensions={1}, to_apply=%bitcast.93.reduce_sub_computation | reduce | bytes 2097154
  480.3 2.1 reshape.423
  482.5 9.8 %all-to-all-start.1 = ((bf16[32,2,8192]{2,1,0:T(2,128)(2,1)}), bf16[32,2,8192]{2,1,0:T(2,128)(2,1)}, u32[]{:S(2)}, u32[]{:S(2)}) async-start(bf16[32,2,8192]{2,1,0:T(2,128)(2,1)} %reshape.423), calls=%async_computation.1 | async-start | bytes 2097152 | tf_op jit(solution)/shard_map/all_to_all | solution.py:107
  495.1 21.8 %all-to-all-done.1 = bf16[32,2,8192]{2,1,0:T(2,128)(2,1)} async-done(((bf16[32,2,8192]{2,1,0:T(2,128)(2,1)}), bf16[32,2,8192]{2,1,0:T(2,128)(2,1)}, u32[]{:S(2)}, u32[]{:S(2)}) %all-to-all-start.1) | async-done | bytes 1048608 | tf_op jit(solution)/shard_map/all_to_all | solution.py:107
  516.8 5.8 %reshape.424 = bf16[4096,1,128]{2,1,0:T(2,128)(2,1)} reshape(bf16[32,2,8192]{2,1,0:T(2,128)(2,1)} %all-to-all-done.1) | data formatting | bytes 2097152
  (116 shorter events, 32.6 us)
Async XLA Ops:
  7.2 177.9 %copy-start = (bf16[1,64,128,128]{3,2,1,0:T(8,128)(2,1)S(1)}, bf16[1,64,128,128]{3,2,1,0:T(8,128)(2,1)}, u32[]{:S(2)}) copy-start(bf16[1,64,128,128]{3,2,1,0:T(8,128)(2,1)} %param.16) | copy-start | bytes 6291460
  7.2 90.8 %all-gather.6.cloned.1.call-start = ((), (), s32[]{:S(2)}) async-start(), calls=%async_computation.6 | async-start | bytes 1081344 | tf_op jit(solution)/shard_map/all_gather | solution.py:51
  8.9 172.4 %all-gather.4.cloned.1.call-start = ((), (), s32[]{:S(2)}) async-start(), calls=%async_computation.5 | async-start | bytes 1081344 | tf_op jit(solution)/shard_map/all_gather | solution.py:50
  10.4 259.9 %all-gather.8.cloned.1.call-start = ((), (), s32[]{:S(2)}) async-start(), calls=%async_computation.7 | async-start | bytes 4325376 | tf_op jit(solution)/shard_map/all_gather | solution.py:91
  18.3 83.5 %copy-start.11 = (s32[64]{0:T(128)}, s32[64]{0:T(128)S(1)}, u32[]{:S(2)}) copy-start(s32[64]{0:T(128)S(1)} %get-tuple-element.20) | copy-start | bytes 772
  18.3 87.3 %copy-start.4 = (s32[64]{0:T(128)}, s32[64]{0:T(128)S(1)}, u32[]{:S(2)}) copy-start(s32[64]{0:T(128)S(1)} %get-tuple-element.33) | copy-start | bytes 772
  105.6 4.6 copy-start.9
  105.7 5.0 copy-start.3
  114.6 0.5 copy-start.13
  114.6 70.4 %copy-start.7 = (pred[64]{0:T(512)(128)(4,1)}, pred[64]{0:T(512)(128)(4,1)S(1)}, u32[]{:S(2)}) copy-start(pred[64]{0:T(512)(128)(4,1)S(1)} %get-tuple-element.38) | copy-start | bytes 196
  270.3 9.2 %copy-start.15 = (s32[64]{0:T(128)S(1)}, s32[64]{0:T(128)}, u32[]{:S(2)}) copy-start(s32[64]{0:T(128)} %get-tuple-element.14) | copy-start | bytes 772
  270.3 9.2 %copy-start.16 = (pred[4]{0:T(512)(128)(4,1)S(1)}, pred[4]{0:T(512)(128)(4,1)}, u32[]{:S(2)}) copy-start(pred[4]{0:T(512)(128)(4,1)} %get-tuple-element.15) | copy-start | bytes 16
  270.3 9.2 %copy-start.17 = (pred[4]{0:T(512)(128)(4,1)S(1)}, pred[4]{0:T(512)(128)(4,1)}, u32[]{:S(2)}) copy-start(pred[4]{0:T(512)(128)(4,1)} %get-tuple-element.17) | copy-start | bytes 16
  288.6 99.5 %all-to-all-start = ((bf16[128,32,512]{0,2,1:T(8,128)(2,1)}), bf16[128,32,512]{0,2,1:T(8,128)(2,1)}, u32[]{:S(2)}, u32[]{:S(2)}) async-start(bf16[128,32,512]{0,2,1:T(8,128)(2,1)} %concatenate.7), calls=%async_computation | async-start | bytes 8388608 | tf_op jit(solution)/shard_map/all_to_all | solution.py:9
  295.3 230.1 %reduce-scatter.3.cloned.1.call-start = ((), (), s32[]{:S(2)}) async-start(), calls=%async_computation.8 | async-start | bytes 2228224 | tf_op jit(solution)/shard_map/reduce_scatter | solution.py:113
  295.4 2.1 copy-start.6
  295.4 2.1 copy-start.8
  302.1 0.7 copy-start.10
  302.1 0.7 copy-start.5
  302.1 223.3 %reduce-scatter.5.cloned.1.call-start = ((), (), s32[]{:S(2)}) async-start(), calls=%async_computation.9 | async-start | bytes 2228224 | tf_op jit(solution)/shard_map/reduce_scatter | solution.py:116
  404.2 0.6 copy-start.14
  437.1 7.0 %copy-start.2 = (bf16[64,128,128]{2,1,0:T(8,128)(2,1)S(1)}, bf16[64,128,128]{2,1,0:T(8,128)(2,1)}, u32[]{:S(2)}) copy-start(bf16[64,128,128]{2,1,0:T(8,128)(2,1)} %gather_fusion.4) | copy-start | bytes 6291460
  438.3 44.2 %all-to-all-start.2 = ((bf16[32,2,8192]{2,1,0:T(2,128)(2,1)}), bf16[32,2,8192]{2,1,0:T(2,128)(2,1)S(1)}, u32[]{:S(2)}, u32[]{:S(2)}) async-start(bf16[32,2,8192]{2,1,0:T(2,128)(2,1)} %reshape.425), calls=%async_computation.2 | async-start | bytes 2097152 | tf_op jit(solution)/shard_map/all_to_all | solution.py:108
  444.2 2.4 copy-start.12
  482.5 34.4 %all-to-all-start.1 = ((bf16[32,2,8192]{2,1,0:T(2,128)(2,1)}), bf16[32,2,8192]{2,1,0:T(2,128)(2,1)}, u32[]{:S(2)}, u32[]{:S(2)}) async-start(bf16[32,2,8192]{2,1,0:T(2,128)(2,1)} %reshape.423), calls=%async_computation.1 | async-start | bytes 2097152 | tf_op jit(solution)/shard_map/all_to_all | solution.py:107
  522.6 2.8 copy-start.1
Sparse Core Ops, SparseCore 0:
  11.8 86.1 all-gather.5
  101.7 79.5 all-gather.3
  185.0 85.2 all-gather.7
  302.2 64.3 reduce-scatter.2
  404.4 58.2 reduce-scatter.4
